TPU v7x, 512 devices: a whole 4x4x16 slice. The times are simulated.
512 devices in a mesh: gz: 32 (over z, core), gy: 4 (over y), gx: 4 (over x).
Axes of the slice: x: 4, y: 4, z: 16, core: 2. Of those that a mesh axis runs over, the one named last changes fastest.
Arguments:
- pressure: float32 [128, 512, 512], P('gz', 'gy', 'gx'), may hold values from -6 to 6
- light: float32 [4, 3], replicated, may hold values from -4 to 4
- palette: float32 [3, 2], replicated, may hold values from -4 to 4
- rate: float32 [4], replicated, may hold values from 0.00390625 to 0.0234375
- shear: int32 [4, 128, 2], replicated, may hold values from 0 to 8
- offset: int32 [4, 32, 2], replicated, may hold values from 0 to 31
- order: int32 [4, 32], replicated, may hold values from 0 to 31, each once within a row
Outputs:
- picture: float32 [4, 4, 32, 16, 512], P(None, None, 'gz', 'gy', 'gx')
Inputs may be any that keep to these rules, and one draw needn't show every extreme that they name: `order`: each row is a permutation of 0 to 31.
All inputs are finite; a program needn't handle non-finite values.
Results may differ from a plain program's by a relative error of at most 0.00005.
Values sent between devices are 32-bit elements; how exact they have to be, the bound alone decides.
No kernel may reach another device: no remote copies, remote signals or barrier semaphores. Data moves between devices by JAX's collectives and lax.ppermute only.
A program may use at most 64 MiB of HBM per device.

v0:
```python
import jax
import jax.numpy as jnp
from jax import lax
from jax.sharding import PartitionSpec as P

VIEWS = 4
SHEAR = 8
REACH = 32


def padded(cells, sides, width):
    for axis, dim in sides:
        count = lax.axis_size(axis)
        ends = count - 1
        head = lax.slice_in_dim(cells, 0, width, axis=dim)
        tail = lax.slice_in_dim(cells, cells.shape[dim] - width, cells.shape[dim], axis=dim)
        cells = jnp.concatenate(
            [
                lax.ppermute(tail, axis, [(i, (i + 1) % count) for i in range(ends)]),
                cells,
                lax.ppermute(head, axis, [((i + 1) % count, i) for i in range(ends)]),
            ],
            axis=dim,
        )
    return cells


def shifted(value, axis, steps):
    count = lax.axis_size(axis)
    first, last = (max(0, -steps), min(count, count - steps))
    return lax.ppermute(value, axis, [(source, source + steps) for source in range(first, last)])


def surface_terms(slab):
    inner = slab[1:-1, 1:-1, 1:-1]
    grad_depth = 0.5 * (slab[2:, 1:-1, 1:-1] - slab[:-2, 1:-1, 1:-1])
    grad_rows = 0.5 * (slab[1:-1, 2:, 1:-1] - slab[1:-1, :-2, 1:-1])
    grad_cols = 0.5 * (slab[1:-1, 1:-1, 2:] - slab[1:-1, 1:-1, :-2])
    factor = lax.rsqrt(
        grad_depth * grad_depth + grad_rows * grad_rows + grad_cols * grad_cols + 1.0
    )
    return (inner, (grad_depth * factor, grad_rows * factor, grad_cols * factor))


def render_layers(inner, normals, shifts, light, palette, rate, rows, cols):
    lengths = jnp.sqrt(jnp.sum(light * light, axis=1, keepdims=True) + 1.0)
    towards = light / lengths
    offsets = palette[:, 0][:, None, None]
    slopes = palette[:, 1][:, None, None]
    layers = []
    for view in range(light.shape[0]):

        def advance(carry, items):
            color, depth = carry
            value_slab, normal_depth, normal_rows, normal_cols, moved = items
            start = (SHEAR - moved[0], SHEAR - moved[1])
            value = lax.dynamic_slice(value_slab, start, (rows, cols))
            dot = (
                lax.dynamic_slice(normal_depth, start, (rows, cols)) * towards[view, 0]
                + lax.dynamic_slice(normal_rows, start, (rows, cols)) * towards[view, 1]
                + lax.dynamic_slice(normal_cols, start, (rows, cols)) * towards[view, 2]
            )
            shade = 0.25 + 0.75 * dot * dot
            density = rate[view] * (1.0 + jnp.tanh(value))
            alpha = 1.0 - jnp.exp(-density)
            weight = alpha * jnp.exp(-depth)
            hues = jax.nn.sigmoid(offsets + slopes * value[None]) * shade[None]
            return ((color + hues * weight[None], depth + density), None)

        start_carry = (
            jnp.zeros((3, rows, cols), jnp.float32),
            jnp.zeros((rows, cols), jnp.float32),
        )
        (color, depth), _ = lax.scan(
            advance, start_carry, (inner, normals[0], normals[1], normals[2], shifts[view])
        )
        layers.append(jnp.concatenate([color, depth[None]], axis=0))
    return jnp.stack(layers)


def precedence(order):
    bricks = order.shape[1]
    onehot = (order[:, :, None] == jnp.arange(bricks, dtype=jnp.int32)[None, None, :]).astype(
        jnp.float32
    )
    ranks = jnp.sum(onehot * jnp.arange(bricks, dtype=jnp.float32)[None, :, None], axis=1)
    return (ranks[:, None, :] < ranks[:, :, None]).astype(jnp.float32)


def on_device(pressure, light, palette, rate, shear, offset, order):
    depth_cells, rows, cols = pressure.shape
    brick = lax.axis_index("gz")
    zero = jnp.zeros((), jnp.int32)
    widened = padded(pressure, (("gy", 1), ("gx", 2)), SHEAR + 1)
    slab = padded(widened, (("gz", 0),), 1)
    inner, normals = surface_terms(slab)
    shifts = lax.dynamic_slice(shear, (zero, brick * depth_cells, zero), (VIEWS, depth_cells, 2))
    layers = render_layers(inner, normals, shifts, light, palette, rate, rows, cols)
    moved = lax.dynamic_index_in_dim(offset, brick, 1, keepdims=False)
    blank = jnp.zeros((4, rows + REACH, cols + REACH), jnp.float32)
    canvas = jnp.stack(
        [
            lax.dynamic_update_slice(blank, layers[view], (zero, moved[view, 0], moved[view, 1]))
            for view in range(VIEWS)
        ]
    )
    own_tile = canvas[:, :, :rows, :cols]
    from_above = shifted(canvas[:, :, rows:, :cols], "gy", 1)
    from_left = shifted(canvas[:, :, :rows, cols:], "gx", 1)
    from_diagonal = shifted(canvas[:, :, rows:, cols:], ("gy", "gx"), lax.axis_size("gx") + 1)
    from_diagonal = from_diagonal * (lax.axis_index("gx") > 0).astype(jnp.float32)
    own_tile = own_tile.at[:, :, :REACH, :].add(from_above)
    own_tile = own_tile.at[:, :, :, :REACH].add(from_left)
    own_tile = own_tile.at[:, :, :REACH, :REACH].add(from_diagonal)
    ranking = precedence(order)
    pieces = lax.all_to_all(own_tile[None], "gz", split_axis=3, concat_axis=0, tiled=True)
    depths = pieces[:, :, 3]
    cover = jnp.einsum("vbc,cvyx->bvyx", ranking, depths, precision=lax.Precision.HIGHEST)
    colors = jnp.sum(pieces[:, :, :3] * jnp.exp(-cover)[:, :, None], axis=0)
    opacity = 1.0 - jnp.exp(-jnp.sum(depths, axis=0))
    image = jnp.concatenate([colors, opacity[:, None]], axis=1)
    return image[:, :, None]


def solution(mesh):
    return jax.shard_map(
        on_device,
        mesh=mesh,
        in_specs=(P("gz", "gy", "gx"), P(), P(), P(), P(), P(), P()),
        out_specs=P(None, None, "gz", "gy", "gx"),
        check_vma=False,
    )
```

profile of v0, /device:TPU:27, one launch (start us, length us, event | category | flops | bytes accessed | tf_op | source)
XLA Modules:
  0.0 283.3 jit_solution(8438812857838250541)
XLA Ops:
  0.8 2.4 collective-permute-start.1
  9.0 2.2 collective-permute-start.3
  11.2 3.1 %collective-permute-start.2 = (f32[4,146,9]{2,1,0:T(8,128)S(1)}, f32[4,146,9]{2,1,0:T(8,128)S(1)}, u32[]{:S(2)}, u32[]{:S(2)}) collective-permute-start(f32[4,146,9]{2,1,0:T(8,128)S(1)} %get-tuple-element.1120), channel_id=1, source_target_pairs={{0,1},{1,2},{2,3},{4,5},{5,6},{6,7},{8,9},{9,10},{10,11},{12,13},{... | collective-permute-start | bytes 63080 | tf_op jit(solution)/shard_map/ppermute | solution.py:19
  31.5 6.2 %collective-permute-start.5 = (f32[1,146,146]{2,1,0:T(8,128)S(1)}, f32[1,146,146]{2,1,0:T(8,128)S(1)}, u32[]{:S(2)}, u32[]{:S(2)}) collective-permute-start(f32[1,146,146]{2,1,0:T(8,128)S(1)} %get-tuple-element.1118), channel_id=1, source_target_pairs={{0,16},{16,32},{32,48},{48,64},{64,80},{80,96},{96,112},{112,128},... | collective-permute-start | bytes 255800 | tf_op jit(solution)/shard_map/ppermute | solution.py:19
  39.9 4.4 %collective-permute-done.4 = f32[1,146,146]{2,1,0:T(8,128)S(1)} collective-permute-done((f32[1,146,146]{2,1,0:T(8,128)S(1)}, f32[1,146,146]{2,1,0:T(8,128)S(1)}, u32[]{:S(2)}, u32[]{:S(2)}) %collective-permute-start.4) | collective-permute-done | bytes 85296 | tf_op jit(solution)/shard_map/ppermute | solution.py:21
  45.4 2.4 fusion.19
  47.8 31.7 %while.70 = (s32[]{:T(128)}, f32[3,128,128]{2,1,0:T(8,128)S(1)}, f32[128,128]{1,0:T(8,128)S(1)}, f32[3,1,1]{0,2,1:T(1,128)S(1)}, f32[3,1,1]{0,2,1:T(1,128)S(1)},...) while((s32[]{:T(128)}, f32[3,128,128]{2,1,0:T(8,128)S(1)}, ...), condition=%wide.region_8.9_spmd.clone, body=%wide.region_7.8_spmd.clone.sunk | while | flops 753678 | bytes 1442253 | solution.py:74
  53.6 2.0 fusion.65
  61.5 2.0 fusion.65
  69.4 2.0 fusion.65
  77.3 2.0 fusion.65
  79.5 31.0 %while.69 = (s32[]{:T(128)}, f32[3,128,128]{2,1,0:T(8,128)S(1)}, f32[128,128]{1,0:T(8,128)S(1)}, f32[3,1,1]{0,2,1:T(1,128)S(1)}, f32[3,1,1]{0,2,1:T(1,128)S(1)},...) while((s32[]{:T(128)}, f32[3,128,128]{2,1,0:T(8,128)S(1)}, ...), condition=%wide.region_6.7_spmd.clone, body=%wide.region_5.6_spmd.clone.sunk | while | flops 753678 | bytes 1442253 | solution.py:74
  85.1 1.9 fusion.62
  92.8 1.9 fusion.62
  100.6 1.9 fusion.62
  108.3 1.9 fusion.62
  110.5 31.0 %while.68 = (s32[]{:T(128)}, f32[3,128,128]{2,1,0:T(8,128)S(1)}, f32[128,128]{1,0:T(8,128)S(1)}, f32[3,1,1]{0,2,1:T(1,128)S(1)}, f32[3,1,1]{0,2,1:T(1,128)S(1)},...) while((s32[]{:T(128)}, f32[3,128,128]{2,1,0:T(8,128)S(1)}, ...), condition=%wide.region_4.5_spmd.clone, body=%wide.region_3.4_spmd.clone.sunk | while | flops 753678 | bytes 1442253 | solution.py:74
  116.1 1.9 fusion.59
  123.8 1.9 fusion.59
  131.6 1.9 fusion.59
  141.4 24.5 %while.67 = (s32[]{:T(128)}, f32[3,128,128]{2,1,0:T(8,128)S(1)}, f32[128,128]{1,0:T(8,128)S(1)}, f32[3,1,1]{0,2,1:T(1,128)S(1)}, f32[3,1,1]{0,2,1:T(1,128)S(1)},...) while((s32[]{:T(128)}, f32[3,128,128]{2,1,0:T(8,128)S(1)}, ...), condition=%wide.region_2.3_spmd.clone, body=%wide.region_1.2_spmd.clone.sunk | while | flops 753678 | bytes 1442245 | solution.py:74
  157.7 1.9 fusion.56
  166.1 3.1 %dynamic_update_slice.19 = f32[1,4,160,160]{3,2,1,0:T(8,128)S(1)} dynamic-update-slice(f32[1,4,160,160]{3,2,1,0:T(8,128)S(1)} %broadcast_in_dim.30.clone, f32[1,4,128,128]{3,2,1,0:T(8,128)S(1)} %maximum_bitcast_fusion.3, s32[]{:T(128)} %constant.961.clone.1, s32[]{:T(128)} %constant.961.clone.1, s32[]{:T(128)S(6)} %select_n.135, s32[]{:T(128)S(6)} %select_n.136) | dynamic-update-slice | bytes 524292 | tf_op jit(solution)/shard_map/dynamic_update_slice | solution.py:103
  169.3 3.1 %dynamic_update_slice.18 = f32[1,4,160,160]{3,2,1,0:T(8,128)S(1)} dynamic-update-slice(f32[1,4,160,160]{3,2,1,0:T(8,128)S(1)} %broadcast_in_dim.30.clone.1, f32[1,4,128,128]{3,2,1,0:T(8,128)S(1)} %maximum_bitcast_fusion.2, s32[]{:T(128)} %constant.961.clone.1, s32[]{:T(128)} %constant.961.clone.1, s32[]{:T(128)S(6)} %select_n.133, s32[]{:T(128)S(6)} %select_n.134) | dynamic-update-slice | bytes 524292 | tf_op jit(solution)/shard_map/dynamic_update_slice | solution.py:103
  172.5 3.1 %dynamic_update_slice.17 = f32[1,4,160,160]{3,2,1,0:T(8,128)S(1)} dynamic-update-slice(f32[1,4,160,160]{3,2,1,0:T(8,128)S(1)} %broadcast_in_dim.30.clone.2, f32[1,4,128,128]{3,2,1,0:T(8,128)S(1)} %maximum_bitcast_fusion.1, s32[]{:T(128)} %constant.961.clone.1, s32[]{:T(128)} %constant.961.clone.1, s32[]{:T(128)S(6)} %select_n.131, s32[]{:T(128)S(6)} %select_n.132) | dynamic-update-slice | bytes 524292 | tf_op jit(solution)/shard_map/dynamic_update_slice | solution.py:103
  175.7 3.1 %dynamic_update_slice.16 = f32[1,4,160,160]{3,2,1,0:T(8,128)S(1)} dynamic-update-slice(f32[1,4,160,160]{3,2,1,0:T(8,128)S(1)} %broadcast_in_dim.30.clone.3, f32[1,4,128,128]{3,2,1,0:T(8,128)S(1)} %maximum_bitcast_fusion, s32[]{:T(128)} %constant.961.clone.1, s32[]{:T(128)} %constant.961.clone.1, s32[]{:T(128)S(6)} %select_n.129, s32[]{:T(128)S(6)} %select_n.130) | dynamic-update-slice | bytes 524292 | tf_op jit(solution)/shard_map/dynamic_update_slice | solution.py:103
  183.1 3.1 %collective-permute-start.7 = (f32[4,4,128,32]{2,3,1,0:T(8,128)S(1)}, f32[4,4,128,32]{2,3,1,0:T(8,128)S(1)}, u32[]{:S(2)}, u32[]{:S(2)}) collective-permute-start(f32[4,4,128,32]{2,3,1,0:T(8,128)S(1)} %copy.32), channel_id=1, source_target_pairs={{0,1},{1,2},{2,3},{4,5},{5,6},{6,7},{8,9},{9,10},{10,11},{12,13},{... | collective-permute-start | bytes 786440 | tf_op jit(solution)/shard_map/ppermute | solution.py:31
  188.3 2.3 slice.439
  194.2 5.9 %collective-permute-done.6 = f32[4,4,32,128]{3,2,1,0:T(8,128)S(1)} collective-permute-done((f32[4,4,32,128]{3,2,1,0:T(8,128)}, f32[4,4,32,128]{3,2,1,0:T(8,128)S(1)}, u32[]{:S(2)}, u32[]{:S(2)}) %collective-permute-start.6) | collective-permute-done | bytes 262176 | tf_op jit(solution)/shard_map/ppermute | solution.py:31
  202.4 2.0 scatter-add.11
  208.1 17.6 %all-to-all-start = ((f32[1,4,4,128,128]{4,2,1,0,3:T(4,128)}), f32[1,4,4,128,128]{4,2,1,0,3:T(4,128)S(1)}, u32[]{:S(2)}, u32[]{:S(2)}) async-start(f32[1,4,4,128,128]{4,2,1,0,3:T(4,128)} %copy.34), calls=%async_computation | async-start | bytes 2097152 | tf_op jit(solution)/shard_map/all_to_all | solution.py:116
  225.9 55.6 %all-to-all-done = f32[1,4,4,128,128]{4,2,1,0,3:T(4,128)S(1)} async-done(((f32[1,4,4,128,128]{4,2,1,0,3:T(4,128)}), f32[1,4,4,128,128]{4,2,1,0,3:T(4,128)S(1)}, u32[]{:S(2)}, u32[]{:S(2)}) %all-to-all-start) | async-done | bytes 1048608 | tf_op jit(solution)/shard_map/all_to_all | solution.py:116
  (210 shorter events, 85.2 us)
Async XLA Ops:
  0.0 6.8 %copy-start = (s32[4,32,2]{1,2,0:T(2,128)S(1)}, s32[4,32,2]{1,2,0:T(2,128)}, u32[]{:S(2)}) copy-start(s32[4,32,2]{1,2,0:T(2,128)} %param.26) | copy-start | bytes 3076
  0.0 44.3 %copy-start.3 = (f32[4,128,128]{2,1,0:T(8,128)S(1)}, f32[4,128,128]{2,1,0:T(8,128)}, u32[]{:S(2)}) copy-start(f32[4,128,128]{2,1,0:T(8,128)} %param.21) | copy-start | bytes 786436
  0.0 39.6 %copy-start.9 = (s32[4,128,2]{1,2,0:T(2,128)S(1)}, s32[4,128,2]{1,2,0:T(2,128)}, u32[]{:S(2)}) copy-start(s32[4,128,2]{1,2,0:T(2,128)} %param.25) | copy-start | bytes 12292
  0.8 6.2 %collective-permute-start.1 = (f32[4,9,128]{2,1,0:T(8,128)S(1)}, f32[4,9,128]{2,1,0:T(8,128)S(1)}, u32[]{:S(2)}, u32[]{:S(2)}) collective-permute-start(f32[4,9,128]{2,1,0:T(8,128)S(1)} %get-tuple-element.1123), channel_id=1, source_target_pairs={{4,0},{8,4},{12,8},{5,1},{9,5},{13,9},{6,2},{10,6},{14,10},{7,3},{... | collective-permute-start | bytes 55304 | tf_op jit(solution)/shard_map/ppermute | solution.py:21
  3.2 4.7 %collective-permute-start = (f32[4,9,128]{2,1,0:T(8,128)S(1)}, f32[4,9,128]{2,1,0:T(8,128)S(1)}, u32[]{:S(2)}, u32[]{:S(2)}) collective-permute-start(f32[4,9,128]{2,1,0:T(8,128)S(1)} %get-tuple-element.1122), channel_id=1, source_target_pairs={{0,4},{4,8},{8,12},{1,5},{5,9},{9,13},{2,6},{6,10},{10,14},{3,7},{... | collective-permute-start | bytes 55304 | tf_op jit(solution)/shard_map/ppermute | solution.py:19
  9.0 20.9 %collective-permute-start.3 = (f32[4,146,9]{2,1,0:T(8,128)S(1)}, f32[4,146,9]{2,1,0:T(8,128)S(1)}, u32[]{:S(2)}, u32[]{:S(2)}) collective-permute-start(f32[4,146,9]{2,1,0:T(8,128)S(1)} %get-tuple-element.1121), channel_id=1, source_target_pairs={{1,0},{2,1},{3,2},{5,4},{6,5},{7,6},{9,8},{10,9},{11,10},{13,12},{... | collective-permute-start | bytes 63080 | tf_op jit(solution)/shard_map/ppermute | solution.py:21
  11.2 18.8 %collective-permute-start.2 = (f32[4,146,9]{2,1,0:T(8,128)S(1)}, f32[4,146,9]{2,1,0:T(8,128)S(1)}, u32[]{:S(2)}, u32[]{:S(2)}) collective-permute-start(f32[4,146,9]{2,1,0:T(8,128)S(1)} %get-tuple-element.1120), channel_id=1, source_target_pairs={{0,1},{1,2},{2,3},{4,5},{5,6},{6,7},{8,9},{9,10},{10,11},{12,13},{... | collective-permute-start | bytes 63080 | tf_op jit(solution)/shard_map/ppermute | solution.py:19
  29.9 15.4 %copy-start.6 = (f32[4,146,9]{2,1,0:T(8,128)}, f32[4,146,9]{2,1,0:T(8,128)S(1)}, u32[]{:S(2)}) copy-start(f32[4,146,9]{2,1,0:T(8,128)S(1)} %collective-permute-done.3) | copy-start | bytes 63076
  29.9 15.4 %copy-start.7 = (f32[4,146,9]{2,1,0:T(8,128)}, f32[4,146,9]{2,1,0:T(8,128)S(1)}, u32[]{:S(2)}) copy-start(f32[4,146,9]{2,1,0:T(8,128)S(1)} %collective-permute-done.2) | copy-start | bytes 63076
  31.4 14.0 %copy-start.4 = (f32[4,128,128]{2,1,0:T(8,128)S(1)}, f32[4,128,128]{2,1,0:T(8,128)}, u32[]{:S(2)}) copy-start(f32[4,128,128]{2,1,0:T(8,128)} %param.21) | copy-start | bytes 786436
  31.5 8.4 %collective-permute-start.5 = (f32[1,146,146]{2,1,0:T(8,128)S(1)}, f32[1,146,146]{2,1,0:T(8,128)S(1)}, u32[]{:S(2)}, u32[]{:S(2)}) collective-permute-start(f32[1,146,146]{2,1,0:T(8,128)S(1)} %get-tuple-element.1118), channel_id=1, source_target_pairs={{0,16},{16,32},{32,48},{48,64},{64,80},{80,96},{96,112},{112,128},... | collective-permute-start | bytes 255800 | tf_op jit(solution)/shard_map/ppermute | solution.py:19
  37.7 6.5 %collective-permute-start.4 = (f32[1,146,146]{2,1,0:T(8,128)S(1)}, f32[1,146,146]{2,1,0:T(8,128)S(1)}, u32[]{:S(2)}, u32[]{:S(2)}) collective-permute-start(f32[1,146,146]{2,1,0:T(8,128)S(1)} %get-tuple-element.1117), channel_id=1, source_target_pairs={{16,0},{32,16},{48,32},{64,48},{80,64},{96,80},{112,96},{128,112},... | collective-permute-start | bytes 255800 | tf_op jit(solution)/shard_map/ppermute | solution.py:21
  45.4 2.4 copy-start.8
  179.1 1.5 copy-start.2
  183.1 9.7 %collective-permute-start.7 = (f32[4,4,128,32]{2,3,1,0:T(8,128)S(1)}, f32[4,4,128,32]{2,3,1,0:T(8,128)S(1)}, u32[]{:S(2)}, u32[]{:S(2)}) collective-permute-start(f32[4,4,128,32]{2,3,1,0:T(8,128)S(1)} %copy.32), channel_id=1, source_target_pairs={{0,1},{1,2},{2,3},{4,5},{5,6},{6,7},{8,9},{9,10},{10,11},{12,13},{... | collective-permute-start | bytes 786440 | tf_op jit(solution)/shard_map/ppermute | solution.py:31
  187.0 13.1 %collective-permute-start.6 = (f32[4,4,32,128]{3,2,1,0:T(8,128)}, f32[4,4,32,128]{3,2,1,0:T(8,128)S(1)}, u32[]{:S(2)}, u32[]{:S(2)}) collective-permute-start(f32[4,4,32,128]{3,2,1,0:T(8,128)} %pad_maximum_fusion.14), channel_id=1, source_target_pairs={{0,4},{4,8},{8,12},{1,5},{5,9},{9,13},{2,6},{6,10},{10,14},{3,7},{... | collective-permute-start | bytes 786440 | tf_op jit(solution)/shard_map/ppermute | solution.py:31
  191.4 13.1 %collective-permute-start.8 = (f32[4,4,32,32]{3,2,1,0:T(8,128)}, f32[4,4,32,32]{3,2,1,0:T(8,128)}, u32[]{:S(2)}, u32[]{:S(2)}) collective-permute-start(f32[4,4,32,32]{3,2,1,0:T(8,128)} %pad_maximum_fusion.13), channel_id=1, source_target_pairs={{0,5},{1,6},{2,7},{3,8},{4,9},{5,10},{6,11},{7,12},{8,13},{9,14},{... | collective-permute-start | bytes 196616 | tf_op jit(solution)/shard_map/ppermute | solution.py:31
  194.2 6.7 %copy-start.5 = (f32[4,4,128,32]{3,2,1,0:T(8,128)S(1)}, f32[4,4,128,32]{3,2,1,0:T(8,128)}, u32[]{:S(2)}) copy-start(f32[4,4,128,32]{3,2,1,0:T(8,128)} %copy.33) | copy-start | bytes 786436
  200.8 1.5 copy-start.1
  204.4 21.4 %copy-start.10 = (s32[4,32]{1,0:T(4,128)S(1)}, s32[4,32]{1,0:T(4,128)}, u32[]{:S(2)}) copy-start(s32[4,32]{1,0:T(4,128)} %param.27) | copy-start | bytes 1540
  208.1 73.3 %all-to-all-start = ((f32[1,4,4,128,128]{4,2,1,0,3:T(4,128)}), f32[1,4,4,128,128]{4,2,1,0,3:T(4,128)S(1)}, u32[]{:S(2)}, u32[]{:S(2)}) async-start(f32[1,4,4,128,128]{4,2,1,0,3:T(4,128)} %copy.34), calls=%async_computation | async-start | bytes 2097152 | tf_op jit(solution)/shard_map/all_to_all | solution.py:116
where the time goes:
time: 285 us; the launch traced here: 283 us
  waiting for transfers between devices  66.9 us (23%)
  other arithmetic  64.2 us (23%)
  local copies, waits for them, and re-layouts  56.4 us (20%)
  starting transfers between devices  40.6 us (14%)
  loops' own time  39.5 us (14%)
  between operations  15.4 us (5%)
    all_to_all x1, waiting for transfers between devices, on_device(): lax.all_to_all(own_tile[None], 'gz', split_axis=3, concat_axis=0, tiled=T...  55.6 us
    another operation x4, loops' own time, render_layers(): lax.scan(advance, start_carry, (inner, normals[0], normals[1], normals[2]...  39.5 us
    mul x16, other arithmetic, advance(): hues = jax.nn.sigmoid(offsets + slopes * value[None]) * shade[None]  31.1 us
    all_to_all x1, starting transfers between devices, on_device(): lax.all_to_all(own_tile[None], 'gz', split_axis=3, concat_axis=0, tiled=T...  17.6 us
    dynamic_update_slice x4, local copies, waits for them, and re-layouts, on_device(): lax.dynamic_update_slice(blank, layers[view], (zero, moved[view, 0], move...  12.5 us
    add x32, other arithmetic, advance(): return ((color + hues * weight[None], depth + density), None)  11.8 us
    ppermute x3, starting transfers between devices, padded(): lax.ppermute(tail, axis, [(i, (i + 1) % count) for i in range(ends)])  10.6 us
    slice x16, local copies, waits for them, and re-layouts, advance(): towards[view, 0]  9.97 us
  transfers between devices with their start and end apart: 10, of which 5 were waited for; matrix products, arithmetic and copies ran while one was open for 4% of the time, Pallas kernels for 0%

commit v1 on v0

--- a/solution.py
+++ b/solution.py
@@ -1,11 +1,23 @@
+import functools
 import jax
 import jax.numpy as jnp
 from jax import lax
 from jax.sharding import PartitionSpec as P
+from jax.lax import all_to_all, axis_size
 
 VIEWS = 4
 SHEAR = 8
 REACH = 32
+
+
+def _tell_regions(a0, ndim_at, dimension_no):
+    return jnp.concatenate(
+        all_to_all(jnp.stack(jnp.split(a0, axis_size("gz"), axis=ndim_at)), "gz", 0, 0),
+        axis=dimension_no,
+    )
+
+
+load_sectors_on = functools.partial(_tell_regions, ndim_at=3, dimension_no=0)
 
 
 def padded(cells, sides, width):
@@ -113,7 +125,7 @@
     own_tile = own_tile.at[:, :, :, :REACH].add(from_left)
     own_tile = own_tile.at[:, :, :REACH, :REACH].add(from_diagonal)
     ranking = precedence(order)
-    pieces = lax.all_to_all(own_tile[None], "gz", split_axis=3, concat_axis=0, tiled=True)
+    pieces = load_sectors_on(own_tile[None])
     depths = pieces[:, :, 3]
     cover = jnp.einsum("vbc,cvyx->bvyx", ranking, depths, precision=lax.Precision.HIGHEST)
     colors = jnp.sum(pieces[:, :, :3] * jnp.exp(-cover)[:, :, None], axis=0)

time: 285 us -> 286 us (level)
  no operation moved by 1% of the time
where the time goes in v1:
time: 286 us; the launch traced here: 284 us
  waiting for transfers between devices  66.9 us (23%)
  other arithmetic  64.2 us (22%)
  local copies, waits for them, and re-layouts  56.6 us (20%)
  starting transfers between devices  40.6 us (14%)
  loops' own time  39.5 us (14%)
  between operations  15.5 us (5%)
    all_to_all x1, waiting for transfers between devices, _tell_regions(): all_to_all(jnp.stack(jnp.split(a0, axis_size('gz'), axis=ndim_at)), 'gz',...  55.6 us
    another operation x4, loops' own time, render_layers(): lax.scan(advance, start_carry, (inner, normals[0], normals[1], normals[2]...  39.5 us
    mul x16, other arithmetic, advance(): hues = jax.nn.sigmoid(offsets + slopes * value[None]) * shade[None]  31.1 us
    all_to_all x1, starting transfers between devices, _tell_regions(): all_to_all(jnp.stack(jnp.split(a0, axis_size('gz'), axis=ndim_at)), 'gz',...  17.6 us
    dynamic_update_slice x4, local copies, waits for them, and re-layouts, on_device(): lax.dynamic_update_slice(blank, layers[view], (zero, moved[view, 0], move...  12.5 us
    add x32, other arithmetic, advance(): return ((color + hues * weight[None], depth + density), None)  11.8 us
    ppermute x3, starting transfers between devices, padded(): lax.ppermute(tail, axis, [(i, (i + 1) % count) for i in range(ends)])  10.6 us
    slice x16, local copies, waits for them, and re-layouts, advance(): towards[view, 0]  9.97 us
  transfers between devices with their start and end apart: 10, of which 5 were waited for; matrix products, arithmetic and copies ran while one was open for 4% of the time, Pallas kernels for 0%

profile of v1, /device:TPU:27, one launch (start us, length us, event | category | flops | bytes accessed | tf_op | source)
XLA Modules:
  0.0 283.6 jit_solution(18301825607352440245)
XLA Ops:
  0.8 2.4 collective-permute-start.1
  9.0 2.2 collective-permute-start.3
  11.2 3.1 %collective-permute-start.2 = (f32[4,146,9]{2,1,0:T(8,128)S(1)}, f32[4,146,9]{2,1,0:T(8,128)S(1)}, u32[]{:S(2)}, u32[]{:S(2)}) collective-permute-start(f32[4,146,9]{2,1,0:T(8,128)S(1)} %get-tuple-element.1120), channel_id=1, source_target_pairs={{0,1},{1,2},{2,3},{4,5},{5,6},{6,7},{8,9},{9,10},{10,11},{12,13},{... | collective-permute-start | bytes 63080 | tf_op jit(solution)/shard_map/ppermute | solution.py:31
  31.5 6.2 %collective-permute-start.5 = (f32[1,146,146]{2,1,0:T(8,128)S(1)}, f32[1,146,146]{2,1,0:T(8,128)S(1)}, u32[]{:S(2)}, u32[]{:S(2)}) collective-permute-start(f32[1,146,146]{2,1,0:T(8,128)S(1)} %get-tuple-element.1118), channel_id=1, source_target_pairs={{0,16},{16,32},{32,48},{48,64},{64,80},{80,96},{96,112},{112,128},... | collective-permute-start | bytes 255800 | tf_op jit(solution)/shard_map/ppermute | solution.py:31
  39.9 4.4 %collective-permute-done.4 = f32[1,146,146]{2,1,0:T(8,128)S(1)} collective-permute-done((f32[1,146,146]{2,1,0:T(8,128)S(1)}, f32[1,146,146]{2,1,0:T(8,128)S(1)}, u32[]{:S(2)}, u32[]{:S(2)}) %collective-permute-start.4) | collective-permute-done | bytes 85296 | tf_op jit(solution)/shard_map/ppermute | solution.py:33
  45.4 2.4 fusion.19
  47.8 31.7 %while.70 = (s32[]{:T(128)}, f32[3,128,128]{2,1,0:T(8,128)S(1)}, f32[128,128]{1,0:T(8,128)S(1)}, f32[3,1,1]{0,2,1:T(1,128)S(1)}, f32[3,1,1]{0,2,1:T(1,128)S(1)},...) while((s32[]{:T(128)}, f32[3,128,128]{2,1,0:T(8,128)S(1)}, ...), condition=%wide.region_8.9_spmd.clone, body=%wide.region_7.8_spmd.clone.sunk | while | flops 753678 | bytes 1442253 | solution.py:86
  53.6 2.0 fusion.65
  61.5 2.0 fusion.65
  69.4 2.0 fusion.65
  77.3 2.0 fusion.65
  79.5 31.0 %while.69 = (s32[]{:T(128)}, f32[3,128,128]{2,1,0:T(8,128)S(1)}, f32[128,128]{1,0:T(8,128)S(1)}, f32[3,1,1]{0,2,1:T(1,128)S(1)}, f32[3,1,1]{0,2,1:T(1,128)S(1)},...) while((s32[]{:T(128)}, f32[3,128,128]{2,1,0:T(8,128)S(1)}, ...), condition=%wide.region_6.7_spmd.clone, body=%wide.region_5.6_spmd.clone.sunk | while | flops 753678 | bytes 1442253 | solution.py:86
  85.1 1.9 fusion.62
  92.8 1.9 fusion.62
  100.6 1.9 fusion.62
  108.3 1.9 fusion.62
  110.5 31.0 %while.68 = (s32[]{:T(128)}, f32[3,128,128]{2,1,0:T(8,128)S(1)}, f32[128,128]{1,0:T(8,128)S(1)}, f32[3,1,1]{0,2,1:T(1,128)S(1)}, f32[3,1,1]{0,2,1:T(1,128)S(1)},...) while((s32[]{:T(128)}, f32[3,128,128]{2,1,0:T(8,128)S(1)}, ...), condition=%wide.region_4.5_spmd.clone, body=%wide.region_3.4_spmd.clone.sunk | while | flops 753678 | bytes 1442253 | solution.py:86
  116.1 1.9 fusion.59
  123.8 1.9 fusion.59
  139.3 1.9 fusion.59
  141.4 24.5 %while.67 = (s32[]{:T(128)}, f32[3,128,128]{2,1,0:T(8,128)S(1)}, f32[128,128]{1,0:T(8,128)S(1)}, f32[3,1,1]{0,2,1:T(1,128)S(1)}, f32[3,1,1]{0,2,1:T(1,128)S(1)},...) while((s32[]{:T(128)}, f32[3,128,128]{2,1,0:T(8,128)S(1)}, ...), condition=%wide.region_2.3_spmd.clone, body=%wide.region_1.2_spmd.clone.sunk | while | flops 753678 | bytes 1442245 | solution.py:86
  151.6 1.9 fusion.56
  166.1 3.1 %dynamic_update_slice.19 = f32[1,4,160,160]{3,2,1,0:T(8,128)S(1)} dynamic-update-slice(f32[1,4,160,160]{3,2,1,0:T(8,128)S(1)} %broadcast_in_dim.30.clone, f32[1,4,128,128]{3,2,1,0:T(8,128)S(1)} %maximum_bitcast_fusion.3, s32[]{:T(128)} %constant.961.clone.1, s32[]{:T(128)} %constant.961.clone.1, s32[]{:T(128)S(6)} %select_n.135, s32[]{:T(128)S(6)} %select_n.136) | dynamic-update-slice | bytes 524292 | tf_op jit(solution)/shard_map/dynamic_update_slice | solution.py:115
  169.3 3.1 %dynamic_update_slice.18 = f32[1,4,160,160]{3,2,1,0:T(8,128)S(1)} dynamic-update-slice(f32[1,4,160,160]{3,2,1,0:T(8,128)S(1)} %broadcast_in_dim.30.clone.1, f32[1,4,128,128]{3,2,1,0:T(8,128)S(1)} %maximum_bitcast_fusion.2, s32[]{:T(128)} %constant.961.clone.1, s32[]{:T(128)} %constant.961.clone.1, s32[]{:T(128)S(6)} %select_n.133, s32[]{:T(128)S(6)} %select_n.134) | dynamic-update-slice | bytes 524292 | tf_op jit(solution)/shard_map/dynamic_update_slice | solution.py:115
  172.5 3.1 %dynamic_update_slice.17 = f32[1,4,160,160]{3,2,1,0:T(8,128)S(1)} dynamic-update-slice(f32[1,4,160,160]{3,2,1,0:T(8,128)S(1)} %broadcast_in_dim.30.clone.2, f32[1,4,128,128]{3,2,1,0:T(8,128)S(1)} %maximum_bitcast_fusion.1, s32[]{:T(128)} %constant.961.clone.1, s32[]{:T(128)} %constant.961.clone.1, s32[]{:T(128)S(6)} %select_n.131, s32[]{:T(128)S(6)} %select_n.132) | dynamic-update-slice | bytes 524292 | tf_op jit(solution)/shard_map/dynamic_update_slice | solution.py:115
  175.7 3.1 %dynamic_update_slice.16 = f32[1,4,160,160]{3,2,1,0:T(8,128)S(1)} dynamic-update-slice(f32[1,4,160,160]{3,2,1,0:T(8,128)S(1)} %broadcast_in_dim.30.clone.3, f32[1,4,128,128]{3,2,1,0:T(8,128)S(1)} %maximum_bitcast_fusion, s32[]{:T(128)} %constant.961.clone.1, s32[]{:T(128)} %constant.961.clone.1, s32[]{:T(128)S(6)} %select_n.129, s32[]{:T(128)S(6)} %select_n.130) | dynamic-update-slice | bytes 524292 | tf_op jit(solution)/shard_map/dynamic_update_slice | solution.py:115
  183.1 3.1 %collective-permute-start.7 = (f32[4,4,128,32]{2,3,1,0:T(8,128)S(1)}, f32[4,4,128,32]{2,3,1,0:T(8,128)S(1)}, u32[]{:S(2)}, u32[]{:S(2)}) collective-permute-start(f32[4,4,128,32]{2,3,1,0:T(8,128)S(1)} %copy.91), channel_id=1, source_target_pairs={{0,1},{1,2},{2,3},{4,5},{5,6},{6,7},{8,9},{9,10},{10,11},{12,13},{... | collective-permute-start | bytes 786440 | tf_op jit(solution)/shard_map/ppermute | solution.py:43
  188.3 2.3 slice.439
  194.2 5.9 %collective-permute-done.6 = f32[4,4,32,128]{3,2,1,0:T(8,128)S(1)} collective-permute-done((f32[4,4,32,128]{3,2,1,0:T(8,128)}, f32[4,4,32,128]{3,2,1,0:T(8,128)S(1)}, u32[]{:S(2)}, u32[]{:S(2)}) %collective-permute-start.6) | collective-permute-done | bytes 262176 | tf_op jit(solution)/shard_map/ppermute | solution.py:43
  202.4 2.0 scatter-add.11
  208.4 17.6 %all-to-all-start = ((f32[32,1,4,4,4,128]{5,4,2,3,1,0:T(4,128)}), f32[32,1,4,4,4,128]{5,4,2,3,1,0:T(4,128)S(1)}, u32[]{:S(2)}, u32[]{:S(2)}) async-start(f32[32,1,4,4,4,128]{5,4,2,3,1,0:T(4,128)} %copy.93), calls=%async_computation | async-start | bytes 2097152 | tf_op jit(solution)/shard_map/all_to_all | solution.py:15
  226.1 55.6 %all-to-all-done = f32[32,1,4,4,4,128]{5,4,2,3,1,0:T(4,128)S(1)} async-done(((f32[32,1,4,4,4,128]{5,4,2,3,1,0:T(4,128)}), f32[32,1,4,4,4,128]{5,4,2,3,1,0:T(4,128)S(1)}, u32[]{:S(2)}, u32[]{:S(2)}) %all-to-all-start) | async-done | bytes 1048608 | tf_op jit(solution)/shard_map/all_to_all | solution.py:15
  (242 shorter events, 85.4 us)
Async XLA Ops:
  0.0 6.8 %copy-start = (s32[4,32,2]{1,2,0:T(2,128)S(1)}, s32[4,32,2]{1,2,0:T(2,128)}, u32[]{:S(2)}) copy-start(s32[4,32,2]{1,2,0:T(2,128)} %param.26) | copy-start | bytes 3076
  0.0 44.3 %copy-start.3 = (f32[4,128,128]{2,1,0:T(8,128)S(1)}, f32[4,128,128]{2,1,0:T(8,128)}, u32[]{:S(2)}) copy-start(f32[4,128,128]{2,1,0:T(8,128)} %param.21) | copy-start | bytes 786436
  0.0 39.6 %copy-start.9 = (s32[4,128,2]{1,2,0:T(2,128)S(1)}, s32[4,128,2]{1,2,0:T(2,128)}, u32[]{:S(2)}) copy-start(s32[4,128,2]{1,2,0:T(2,128)} %param.25) | copy-start | bytes 12292
  0.8 6.2 %collective-permute-start.1 = (f32[4,9,128]{2,1,0:T(8,128)S(1)}, f32[4,9,128]{2,1,0:T(8,128)S(1)}, u32[]{:S(2)}, u32[]{:S(2)}) collective-permute-start(f32[4,9,128]{2,1,0:T(8,128)S(1)} %get-tuple-element.1123), channel_id=1, source_target_pairs={{4,0},{8,4},{12,8},{5,1},{9,5},{13,9},{6,2},{10,6},{14,10},{7,3},{... | collective-permute-start | bytes 55304 | tf_op jit(solution)/shard_map/ppermute | solution.py:33
  3.2 4.7 %collective-permute-start = (f32[4,9,128]{2,1,0:T(8,128)S(1)}, f32[4,9,128]{2,1,0:T(8,128)S(1)}, u32[]{:S(2)}, u32[]{:S(2)}) collective-permute-start(f32[4,9,128]{2,1,0:T(8,128)S(1)} %get-tuple-element.1122), channel_id=1, source_target_pairs={{0,4},{4,8},{8,12},{1,5},{5,9},{9,13},{2,6},{6,10},{10,14},{3,7},{... | collective-permute-start | bytes 55304 | tf_op jit(solution)/shard_map/ppermute | solution.py:31
  9.0 20.9 %collective-permute-start.3 = (f32[4,146,9]{2,1,0:T(8,128)S(1)}, f32[4,146,9]{2,1,0:T(8,128)S(1)}, u32[]{:S(2)}, u32[]{:S(2)}) collective-permute-start(f32[4,146,9]{2,1,0:T(8,128)S(1)} %get-tuple-element.1121), channel_id=1, source_target_pairs={{1,0},{2,1},{3,2},{5,4},{6,5},{7,6},{9,8},{10,9},{11,10},{13,12},{... | collective-permute-start | bytes 63080 | tf_op jit(solution)/shard_map/ppermute | solution.py:33
  11.2 18.8 %collective-permute-start.2 = (f32[4,146,9]{2,1,0:T(8,128)S(1)}, f32[4,146,9]{2,1,0:T(8,128)S(1)}, u32[]{:S(2)}, u32[]{:S(2)}) collective-permute-start(f32[4,146,9]{2,1,0:T(8,128)S(1)} %get-tuple-element.1120), channel_id=1, source_target_pairs={{0,1},{1,2},{2,3},{4,5},{5,6},{6,7},{8,9},{9,10},{10,11},{12,13},{... | collective-permute-start | bytes 63080 | tf_op jit(solution)/shard_map/ppermute | solution.py:31
  29.9 15.4 %copy-start.6 = (f32[4,146,9]{2,1,0:T(8,128)}, f32[4,146,9]{2,1,0:T(8,128)S(1)}, u32[]{:S(2)}) copy-start(f32[4,146,9]{2,1,0:T(8,128)S(1)} %collective-permute-done.3) | copy-start | bytes 63076
  29.9 15.4 %copy-start.7 = (f32[4,146,9]{2,1,0:T(8,128)}, f32[4,146,9]{2,1,0:T(8,128)S(1)}, u32[]{:S(2)}) copy-start(f32[4,146,9]{2,1,0:T(8,128)S(1)} %collective-permute-done.2) | copy-start | bytes 63076
  31.4 14.0 %copy-start.4 = (f32[4,128,128]{2,1,0:T(8,128)S(1)}, f32[4,128,128]{2,1,0:T(8,128)}, u32[]{:S(2)}) copy-start(f32[4,128,128]{2,1,0:T(8,128)} %param.21) | copy-start | bytes 786436
  31.5 8.4 %collective-permute-start.5 = (f32[1,146,146]{2,1,0:T(8,128)S(1)}, f32[1,146,146]{2,1,0:T(8,128)S(1)}, u32[]{:S(2)}, u32[]{:S(2)}) collective-permute-start(f32[1,146,146]{2,1,0:T(8,128)S(1)} %get-tuple-element.1118), channel_id=1, source_target_pairs={{0,16},{16,32},{32,48},{48,64},{64,80},{80,96},{96,112},{112,128},... | collective-permute-start | bytes 255800 | tf_op jit(solution)/shard_map/ppermute | solution.py:31
  37.7 6.5 %collective-permute-start.4 = (f32[1,146,146]{2,1,0:T(8,128)S(1)}, f32[1,146,146]{2,1,0:T(8,128)S(1)}, u32[]{:S(2)}, u32[]{:S(2)}) collective-permute-start(f32[1,146,146]{2,1,0:T(8,128)S(1)} %get-tuple-element.1117), channel_id=1, source_target_pairs={{16,0},{32,16},{48,32},{64,48},{80,64},{96,80},{112,96},{128,112},... | collective-permute-start | bytes 255800 | tf_op jit(solution)/shard_map/ppermute | solution.py:33
  45.4 2.4 copy-start.8
  179.1 1.5 copy-start.2
  183.1 9.7 %collective-permute-start.7 = (f32[4,4,128,32]{2,3,1,0:T(8,128)S(1)}, f32[4,4,128,32]{2,3,1,0:T(8,128)S(1)}, u32[]{:S(2)}, u32[]{:S(2)}) collective-permute-start(f32[4,4,128,32]{2,3,1,0:T(8,128)S(1)} %copy.91), channel_id=1, source_target_pairs={{0,1},{1,2},{2,3},{4,5},{5,6},{6,7},{8,9},{9,10},{10,11},{12,13},{... | collective-permute-start | bytes 786440 | tf_op jit(solution)/shard_map/ppermute | solution.py:43
  187.0 13.1 %collective-permute-start.6 = (f32[4,4,32,128]{3,2,1,0:T(8,128)}, f32[4,4,32,128]{3,2,1,0:T(8,128)S(1)}, u32[]{:S(2)}, u32[]{:S(2)}) collective-permute-start(f32[4,4,32,128]{3,2,1,0:T(8,128)} %pad_maximum_fusion.14), channel_id=1, source_target_pairs={{0,4},{4,8},{8,12},{1,5},{5,9},{9,13},{2,6},{6,10},{10,14},{3,7},{... | collective-permute-start | bytes 786440 | tf_op jit(solution)/shard_map/ppermute | solution.py:43
  191.3 13.0 %collective-permute-start.8 = (f32[4,4,32,32]{3,2,1,0:T(8,128)}, f32[4,4,32,32]{3,2,1,0:T(8,128)}, u32[]{:S(2)}, u32[]{:S(2)}) collective-permute-start(f32[4,4,32,32]{3,2,1,0:T(8,128)} %pad_maximum_fusion.13), channel_id=1, source_target_pairs={{0,5},{1,6},{2,7},{3,8},{4,9},{5,10},{6,11},{7,12},{8,13},{9,14},{... | collective-permute-start | bytes 196616 | tf_op jit(solution)/shard_map/ppermute | solution.py:43
  194.2 6.7 %copy-start.5 = (f32[4,4,128,32]{3,2,1,0:T(8,128)S(1)}, f32[4,4,128,32]{3,2,1,0:T(8,128)}, u32[]{:S(2)}) copy-start(f32[4,4,128,32]{3,2,1,0:T(8,128)} %copy.92) | copy-start | bytes 786436
  200.8 1.5 copy-start.1
  206.8 19.2 %copy-start.10 = (s32[4,32]{1,0:T(4,128)S(1)}, s32[4,32]{1,0:T(4,128)}, u32[]{:S(2)}) copy-start(s32[4,32]{1,0:T(4,128)} %param.27) | copy-start | bytes 1540
  208.4 73.3 %all-to-all-start = ((f32[32,1,4,4,4,128]{5,4,2,3,1,0:T(4,128)}), f32[32,1,4,4,4,128]{5,4,2,3,1,0:T(4,128)S(1)}, u32[]{:S(2)}, u32[]{:S(2)}) async-start(f32[32,1,4,4,4,128]{5,4,2,3,1,0:T(4,128)} %copy.93), calls=%async_computation | async-start | bytes 2097152 | tf_op jit(solution)/shard_map/all_to_all | solution.py:15
